TPU v7x, 512 devices: a whole 4x8x8 slice. The times are simulated.
512 devices in a mesh: row: 32 (over z, y_lo, core), col: 16 (over x, y_hi).
Axes of the slice: x: 4, y: 8 (y_hi: 4, y_lo: 2; y = y_hi * 2 + y_lo), z: 8, core: 2. Of those that a mesh axis runs over, the one named last changes fastest.
Arguments:
- points: float32 [65536, 16], P(('row', 'col')), may hold values from -1.7 to 1.7
- lengths: float32 [16], replicated, may hold values from 0.6 to 1.6
- outscale: float32 [1], replicated, may hold values from 0.5 to 2
- jitter: float32 [65536], P(('row', 'col')), may hold values from 0.5 to 2
- solution: float32 [65536, 16], P(('row', 'col')), may hold values from -6 to 6
- residual: float32 [65536, 16], P(('row', 'col')), may hold values from -11.3 to 11.3
- direction: float32 [65536, 16], P(('row', 'col')), may hold values from -11.3 to 11.3
Outputs:
- new_solution: float32 [65536, 16], P(('row', 'col'))
- new_residual: float32 [65536, 16], P(('row', 'col'))
- new_direction: float32 [65536, 16], P(('row', 'col'))
All inputs are finite; a program needn't handle non-finite values.
Results may differ from a plain program's by a relative error of at most 0.000098.
Values sent between devices are 32-bit elements; how exact they have to be, the bound alone decides.
A program may use at most 64 MiB of HBM per device.

v0:
```python
import jax
import jax.numpy as jnp
from jax import lax
from jax.sharding import PartitionSpec as P


def kernel_tile(mine, mine_sq, far_scaled, outscale):
    far_sq = jnp.sum(far_scaled * far_scaled, axis=1)
    cross = jnp.dot(
        mine, far_scaled.T, precision=lax.Precision.HIGHEST, preferred_element_type=jnp.float32
    )
    sqdist = mine_sq[:, None] + far_sq[None, :] - 2.0 * cross
    return outscale[0] * jnp.exp(-0.5 * sqdist)


def make_folder(mine, mine_sq, mine_dir, own_index, shard, outscale):

    def add_piece(totals, pieces, start):
        far_scaled = pieces[0]
        far_dir = pieces[1]
        rows = far_scaled.shape[0]
        block = min(rows, shard)

        def one_block(turn, running):
            offset_rows = turn * block
            block_scaled = lax.dynamic_slice_in_dim(far_scaled, offset_rows, block, 0)
            block_dir = lax.dynamic_slice_in_dim(far_dir, offset_rows, block, 0)
            owner_index = offset_rows // shard
            forward = owner_index >= own_index
            mirrored = owner_index > own_index

            def skip_tile(state):
                return state

            def forward_tile(state):
                kernel = kernel_tile(mine, mine_sq, block_scaled, outscale)
                ahead = state[0] + jnp.dot(
                    kernel,
                    block_dir,
                    precision=lax.Precision.HIGHEST,
                    preferred_element_type=jnp.float32,
                )
                return (ahead, state[1])

            def both_tiles(state):
                kernel = kernel_tile(mine, mine_sq, block_scaled, outscale)
                ahead = state[0] + jnp.dot(
                    kernel,
                    block_dir,
                    precision=lax.Precision.HIGHEST,
                    preferred_element_type=jnp.float32,
                )
                back_part = lax.dot_general(
                    kernel,
                    mine_dir,
                    (((0,), (0,)), ((), ())),
                    precision=lax.Precision.HIGHEST,
                    preferred_element_type=jnp.float32,
                )
                earlier = lax.dynamic_slice_in_dim(state[1], offset_rows, block, 0)
                back_total = lax.dynamic_update_slice_in_dim(
                    state[1], earlier + back_part, offset_rows, 0
                )
                return (ahead, back_total)

            branch_index = forward.astype(jnp.int32) + mirrored.astype(jnp.int32)
            return lax.switch(branch_index, (skip_tile, forward_tile, both_tiles), running)

        return lax.fori_loop(0, rows // block, one_block, totals)

    return add_piece


def per_device(points, lengths, outscale, jitter, solution, residual, direction):
    scaled = points / lengths[None, :]
    shard = scaled.shape[0]
    vectors = direction.shape[1]
    norm_now = lax.psum(jnp.sum(residual * residual, axis=0), ("row", "col"))
    mine, mine_dir = (
        lax.all_gather(scaled, "col", axis=0, tiled=True),
        lax.all_gather(direction, "col", axis=0, tiled=True),
    )
    mine_sq = jnp.sum(mine * mine, axis=1)
    group = lax.axis_size("row")
    starting = (
        jnp.zeros((mine.shape[0], vectors), jnp.float32),
        jnp.zeros((shard * group, vectors), jnp.float32),
    )
    folder = make_folder(mine, mine_sq, mine_dir, lax.axis_index("row"), shard, outscale)
    ahead, back = folder(
        starting,
        (
            lax.all_gather(scaled, "row", axis=0, tiled=True),
            lax.all_gather(direction, "row", axis=0, tiled=True),
        ),
        jnp.int32(0),
    )
    product = lax.psum_scatter(ahead, "col", scatter_dimension=0, tiled=True) + lax.psum_scatter(
        back, "row", scatter_dimension=0, tiled=True
    )
    image = product + jitter[:, None] * direction
    curv = lax.psum(jnp.sum(direction * image, axis=0), ("row", "col"))
    alpha = norm_now / curv
    new_solution = solution + alpha[None, :] * direction
    new_residual = residual - alpha[None, :] * image
    norm_next = lax.psum(jnp.sum(new_residual * new_residual, axis=0), ("row", "col"))
    new_direction = new_residual + (norm_next / norm_now)[None, :] * direction
    return (new_solution, new_residual, new_direction)


def solution(mesh):
    return jax.shard_map(
        per_device,
        mesh=mesh,
        in_specs=(
            P(("row", "col"), None),
            P(),
            P(),
            P(("row", "col")),
            P(("row", "col"), None),
            P(("row", "col"), None),
            P(("row", "col"), None),
        ),
        out_specs=(P(("row", "col"), None), P(("row", "col"), None), P(("row", "col"), None)),
        check_vma=False,
    )
```

profile of v0, /device:TPU:1, one launch (start us, length us, event | category | flops | bytes accessed | tf_op | source)
XLA Modules:
  0.0 709.4 jit_solution(9783318376864798929)
XLA Ops:
  8.0 38.7 %all_gather.14 = f32[2048,16]{0,1:T(8,128)S(1)} all-gather(f32[128,16]{0,1:T(8,128)S(1)} %broadcast_divide_fusion), channel_id=1, replica_groups=mesh['row'=32,'col'=16] {'col'}, dimensions={0}, use_global_device_ids=true | all-gather | bytes 139264 | tf_op jit(solution)/shard_map/all_gather | solution.py:80
  46.6 48.6 %all_gather.12 = f32[4096,16]{0,1:T(8,128)S(1)} all-gather(f32[128,16]{0,1:T(8,128)S(1)} %broadcast_divide_fusion), channel_id=1, replica_groups=mesh['row'=32,'col'=16] {'row'}, dimensions={0}, use_global_device_ids=true | all-gather | bytes 270336 | tf_op jit(solution)/shard_map/all_gather | solution.py:93
  95.3 31.7 %all_gather.13 = f32[4096,16]{0,1:T(8,128)S(1)} all-gather(f32[128,16]{0,1:T(8,128)S(1)} %copy-done.2), channel_id=1, replica_groups=mesh['row'=32,'col'=16] {'row'}, dimensions={0}, use_global_device_ids=true | all-gather | bytes 270336 | tf_op jit(solution)/shard_map/all_gather | solution.py:94
  127.0 31.8 %all_gather.15 = f32[2048,16]{0,1:T(8,128)S(1)} all-gather(f32[128,16]{0,1:T(8,128)S(1)} %copy-done.2), channel_id=1, replica_groups=mesh['row'=32,'col'=16] {'col'}, dimensions={0}, use_global_device_ids=true | all-gather | bytes 139264 | tf_op jit(solution)/shard_map/all_gather | solution.py:81
  158.8 138.7 %while.17 = (s32[]{:T(128)}, f32[2048,16]{0,1:T(8,128)S(1)}, f32[4096,16]{0,1:T(8,128)S(1)}, s32[]{:T(128)}, f32[4096,16]{0,1:T(8,128)S(1)}, /*index=5*/f32[4096...) while((s32[]{:T(128)}, f32[2048,16]{0,1:T(8,128)S(1)}, ...), condition=%wide.region_9.10_spmd, body=%wide.region_3.9_spmd.sunk | while | flops 152344480 | bytes 3753582 | solution.py:69
  159.0 3.7 conditional.2
  162.8 4.4 conditional.2
  167.3 4.4 conditional.2
  171.8 4.4 conditional.2
  176.3 4.4 conditional.2
  180.8 4.4 conditional.2
  180.8 2.6 fusion.7
  185.2 4.4 conditional.2
  185.3 2.6 fusion.7
  189.7 4.4 conditional.2
  189.8 2.6 fusion.7
  194.2 4.4 conditional.2
  198.7 4.4 conditional.2
  203.2 4.4 conditional.2
  207.7 4.4 conditional.2
  212.2 4.4 conditional.2
  216.7 4.4 conditional.2
  221.2 4.4 conditional.2
  225.7 4.4 conditional.2
  225.7 2.6 fusion.7
  230.2 4.4 conditional.2
  230.2 2.6 fusion.7
  234.7 4.4 conditional.2
  234.7 2.6 fusion.7
  239.2 4.4 conditional.2
  243.7 4.4 conditional.2
  248.2 4.4 conditional.2
  252.6 4.4 conditional.2
  257.1 4.4 conditional.2
  261.6 4.4 conditional.2
  266.1 4.4 conditional.2
  266.2 2.6 fusion.7
  270.6 4.4 conditional.2
  270.7 2.6 fusion.7
  275.1 4.4 conditional.2
  279.6 4.4 conditional.2
  284.1 4.4 conditional.2
  288.6 4.4 conditional.2
  293.1 4.4 conditional.2
  299.1 88.2 %reduce-scatter.3.cloned.1.call-done = f32[128,16]{0,1:T(8,128)} async-done(((f32[2048,16]{0,1:T(8,128)}), f32[128,16]{0,1:T(8,128)}) %reduce-scatter.3.cloned.1.call-update) | async-done | bytes 8208 | tf_op jit(solution)/shard_map/reduce_scatter | solution.py:98
  387.3 117.9 %reduce-scatter.5.cloned.1.call-done = f32[128,16]{0,1:T(8,128)} async-done(((f32[4096,16]{0,1:T(8,128)}), f32[128,16]{0,1:T(8,128)}) %reduce-scatter.5.cloned.1.call-update) | async-done | bytes 8208 | tf_op jit(solution)/shard_map/reduce_scatter | solution.py:98
  506.2 100.5 %all-reduce = (f32[16]{0:T(128)S(1)}, f32[16]{0:T(128)S(1)}) all-reduce(f32[16]{0:T(128)S(1)} %multiply_reduce_fusion.5, f32[16]{0:T(128)S(1)} %multiply_reduce_fusion.4), channel_id=1, replica_groups=mesh['row'=32,'col'=16] {'row','col'}, use_global_device_ids=true, to_apply=%region_1.0 | all-reduce | flops 32 | bytes 256 | tf_op jit(solution)/shard_map/psum | solution.py:78
  607.4 94.5 %psum.23 = f32[16]{0:T(128)S(1)} all-reduce(f32[16]{0:T(128)S(1)} %get-tuple-element.335), channel_id=1, replica_groups=mesh['row'=32,'col'=16] {'row','col'}, use_global_device_ids=true, to_apply=%region_15.16 | all-reduce | flops 16 | bytes 128 | tf_op jit(solution)/shard_map/psum | solution.py:106
  (180 shorter events, 118.1 us)
Async XLA Ops:
  7.2 380.2 %reduce-scatter.3.cloned.1.call-start = ((), (), s32[]{:S(2)}) async-start(), calls=%async_computation.2 | async-start | bytes 139264 | tf_op jit(solution)/shard_map/reduce_scatter | solution.py:98
  46.6 48.6 %copy-start.2 = (f32[128,16]{0,1:T(8,128)S(1)}, f32[128,16]{0,1:T(8,128)}, u32[]{:S(2)}) copy-start(f32[128,16]{0,1:T(8,128)} %param.18) | copy-start | bytes 24580
  297.5 0.7 copy-start
  297.5 0.7 copy-start.1
  298.2 207.1 %reduce-scatter.5.cloned.1.call-start = ((), (), s32[]{:S(2)}) async-start(), calls=%async_computation.3 | async-start | bytes 270336 | tf_op jit(solution)/shard_map/reduce_scatter | solution.py:98
  298.2 0.7 copy-start.6
  299.0 206.3 %copy-start.8 = (f32[128]{0:T(128)S(1)}, f32[128]{0:T(128)}, u32[]{:S(2)}) copy-start(f32[128]{0:T(128)} %param.15) | copy-start | bytes 1540
  505.3 101.4 %copy-start.3 = (f32[128,16]{0,1:T(8,128)S(1)}, f32[128,16]{0,1:T(8,128)}, u32[]{:S(2)}) copy-start(f32[128,16]{0,1:T(8,128)} %reduce-scatter.3.cloned.1.call-done) | copy-start | bytes 24580
  505.3 101.4 %copy-start.4 = (f32[128,16]{0,1:T(8,128)S(1)}, f32[128,16]{0,1:T(8,128)}, u32[]{:S(2)}) copy-start(f32[128,16]{0,1:T(8,128)} %reduce-scatter.5.cloned.1.call-done) | copy-start | bytes 24580
  505.3 101.4 %copy-start.7 = (f32[128,16]{0,1:T(8,128)S(1)}, f32[128,16]{0,1:T(8,128)}, u32[]{:S(2)}) copy-start(f32[128,16]{0,1:T(8,128)} %param.16) | copy-start | bytes 24580
  607.4 95.1 %copy-start.5 = (f32[128,16]{0,1:T(8,128)}, f32[128,16]{0,1:T(8,128)S(1)}, u32[]{:S(2)}) copy-start(f32[128,16]{0,1:T(8,128)S(1)} %get-tuple-element.336) | copy-start | bytes 24580
Sparse Core Ops, SparseCore 0:
  298.3 88.9 reduce-scatter.2
  390.3 114.8 reduce-scatter.4
where the time goes:
time: 710 us; the launch traced here: 709 us
  blocking collectives  346 us (49%)
  waiting for transfers between devices  207 us (29%)
  matrix products  133 us (19%)
  between operations  14.1 us (2%)
    reduce_scatter x1, waiting for transfers between devices, per_device(): lax.psum_scatter(back, 'row', scatter_dimension=0, tiled=True)  118 us
    psum x1, blocking collectives, per_device(): norm_now = lax.psum(jnp.sum(residual * residual, axis=0), ('row', 'col'))  100 us
    psum x1, blocking collectives, per_device(): lax.psum(jnp.sum(new_residual * new_residual, axis=0), ('row', 'col'))  94.5 us
    reduce_scatter x1, waiting for transfers between devices, per_device(): lax.psum_scatter(ahead, 'col', scatter_dimension=0, tiled=True)  88.2 us
    dot_general x31, matrix products, kernel_tile(): jnp.dot(mine, far_scaled.T, precision=lax.Precision.HIGHEST, preferred_el...  81.9 us
    all_gather x1, blocking collectives, per_device(): lax.all_gather(scaled, 'row', axis=0, tiled=True)  48.6 us
    all_gather x1, blocking collectives, per_device(): lax.all_gather(scaled, 'col', axis=0, tiled=True)  38.7 us
    all_gather x1, blocking collectives, per_device(): lax.all_gather(direction, 'col', axis=0, tiled=True)  31.8 us
  transfers between devices with their start and end apart: 2, of which 2 were waited for; matrix products, arithmetic and copies ran while one was open for 0% of the time, Pallas kernels for 0%

commit v1 on v0

v1 whole, which is shorter than its diff:
```python
import math

import jax
import jax.numpy as jnp
from jax import lax
from jax.experimental import pallas as pl
from jax.experimental.pallas import tpu as pltpu
from jax.sharding import PartitionSpec as P

MESH = pl.DeviceIdType.MESH
BF = jnp.bfloat16
F32 = jnp.float32
LOG2E = math.log2(math.e)
DEPTH = 128
NEAR = 16
FAR = 32
SHARD = 128
NEAR_PTS = NEAR * SHARD
STEP = 512
STEPS = FAR * SHARD // STEP
SLOTS = STEP // SHARD


def split3(x):
    hi = x.astype(BF)
    rest = x - hi.astype(F32)
    mid = rest.astype(BF)
    low = (rest - mid.astype(F32)).astype(BF)
    return hi, mid, low


def augment(u, near):
    hi, mid, low = split3(u)
    half = -0.5 * jnp.sum(u * u, axis=0, keepdims=True)
    h0, h1, h2 = [part.astype(F32) for part in split3(half)]
    row = lax.broadcasted_iota(jnp.int32, u.shape, 0)
    if near:
        ones = jnp.where((row >= 3) & (row < 6), 1.0, 0.0)
        tail = jnp.where(row == 0, h0, jnp.where(row == 1, h1, jnp.where(row == 2, h2, ones)))
        parts = [hi, hi, mid, mid, hi, low]
    else:
        ones = jnp.where(row < 3, 1.0, 0.0)
        tail = jnp.where(row == 3, h0, jnp.where(row == 4, h1, jnp.where(row == 5, h2, ones)))
        parts = [hi, mid, hi, mid, low, hi]
    return jnp.concatenate(parts + [tail.astype(BF), jnp.zeros_like(hi)], axis=0)


def place():
    r, c = lax.axis_index("row"), lax.axis_index("col")
    x, z, core = c // 4, r // 4, lax.rem(r, 2)
    y = lax.rem(c, 4) * 2 + lax.rem(r // 2, 2)
    return x, y, z, core


def device(x, y, z, core):
    return (z * 4 + lax.rem(y, 2) * 2 + core, x * 4 + y // 2)


def kernel(
    points,
    lengths,
    outscale,
    jitter,
    sol,
    res,
    direction,
    new_sol,
    new_res,
    new_dir,
    near,
    far,
    near_op,
    far_op,
    dir_op,
    partial,
    landed,
    dots_near,
    dots_far,
    near_s,
    near_r,
    far_s,
    far_r,
    back_s,
    back_r,
    one_s,
    one_r,
    two_s,
    two_r,
):
    x, y, z, core = place()

    def near_peer(slot, sign):
        dx, dy = slot // 8, slot % 8
        dy = dy if sign > 0 else (8 - dy) % 8
        return device(lax.rem(x + 2 * dx, 4), lax.rem(y + dy, 8), z, core)

    def far_peer(q, dz):
        xl, co = q // 2, q % 2
        mate = x + xl * (1 - 2 * lax.rem(x, 2))
        return device(mate, y, lax.rem(z + dz, 8), lax.rem(core + co, 2))

    def send(src, dst, ss, rs, peer):
        return pltpu.make_async_remote_copy(
            src_ref=src, dst_ref=dst, send_sem=ss, recv_sem=rs, device_id=peer, device_id_type=MESH
        )

    near_to = [near_peer(s, 1) for s in range(NEAR)]
    near_from = [near_peer(s, -1) for s in range(NEAR)]
    far_to = [far_peer(q, dz) for q in range(4) for dz in range(8)]

    barrier = pltpu.get_barrier_semaphore()
    for peer in near_to[1:] + far_to[1:]:
        pl.semaphore_signal(barrier, inc=1, device_id=peer, device_id_type=MESH)

    eye = lax.broadcasted_iota(jnp.int32, (16, 16), 0) == lax.broadcasted_iota(jnp.int32, (16, 16), 1)
    column = jnp.sum(jnp.where(eye, jnp.broadcast_to(lengths[...], (16, 16)), 0.0), axis=1, keepdims=True)
    mine = points[...] * (math.sqrt(LOG2E) / column)
    near[0] = mine
    far[0, :16] = mine
    far[0, 16:] = direction[...]

    pl.semaphore_wait(barrier, NEAR + FAR - 2)

    order = (4, 3, 5, 2, 6, 1, 7)
    z_copy = {
        dz: send(far.at[0], far.at[dz], far_s.at[dz], far_r.at[dz], far_to[dz]) for dz in order
    }
    mate_copy = [
        send(far.at[dz], far.at[16 + dz], far_s.at[16 + dz], far_r.at[16 + dz], far_to[16]) for dz in range(8)
    ]
    core_copy = [
        send(far.at[k], far.at[k + 8], far_s.at[k + 8], far_r.at[k + 8], far_to[8])
        for k in list(range(8)) + list(range(16, 24))
    ]
    near_copy = [
        send(near.at[0], near.at[s], near_s.at[s], near_r.at[s], near_to[s]) for s in range(1, NEAR)
    ]
    for s in (12, 4, 11, 13, 3, 5, 10, 14, 2, 6, 9, 15, 8, 1, 7):
        near_copy[s - 1].start()
    for dz in order:
        z_copy[dz].start()
    mate_copy[0].start()
    core_copy[0].start()

    def prepare_near(s, carry):
        near_op[:, pl.ds(pl.multiple_of(s * SHARD, SHARD), SHARD)] = augment(near[s], True)
        return carry

    def prepare_far(k, carry):
        here = pl.ds(pl.multiple_of(k * SHARD, SHARD), SHARD)
        far_op[here, :] = augment(far[k, :16], False).T
        d = far[k, 16:]
        hi = d.astype(BF)
        dir_op[:, here] = jnp.concatenate([hi, (d - hi.astype(F32)).astype(BF)], axis=0)
        return carry

    for dz in reversed(order):
        z_copy[dz].wait_recv()
        mate_copy[dz].start()
        core_copy[dz].start()
    lax.fori_loop(0, 8, prepare_far, 0)
    for copy in near_copy:
        copy.wait_recv()
    lax.fori_loop(0, NEAR, prepare_near, 0)

    def step(t, carry):
        @pl.when(t == 2)
        def _():
            for k in range(8):
                core_copy[k].wait_recv()
                mate_copy[k].wait_recv()
                core_copy[8 + k].start()
            lax.fori_loop(8, 24, prepare_far, 0)

        @pl.when(t == 6)
        def _():
            for k in range(8):
                core_copy[8 + k].wait_recv()
            lax.fori_loop(24, 32, prepare_far, 0)

        here = pl.ds(pl.multiple_of(t * STEP, STEP), STEP)
        power = jnp.dot(far_op[here, :], near_op[...], preferred_element_type=F32)
        value = jnp.exp2(power)
        high = value.astype(BF)
        low = (value - high.astype(F32)).astype(BF)
        d = dir_op[:, here]
        a = jnp.dot(d, high, preferred_element_type=F32)
        b = jnp.dot(d[:16], low, preferred_element_type=F32)
        total = a[:16] + (a[16:] + b)
        for s in range(NEAR):
            piece = total[:, s * SHARD : (s + 1) * SHARD]
            partial[s] = jnp.where(t == 0, piece, partial[s] + piece)
        return carry

    lax.fori_loop(0, STEPS, step, 0)

    back_copy = [
        send(partial.at[s], landed.at[s], back_s.at[s], back_r.at[s], near_from[s]) for s in range(1, NEAR)
    ]
    for s in (12, 4, 11, 13, 3, 5, 10, 14, 2, 6, 9, 15, 8, 1, 7):
        back_copy[s - 1].start()
    image = partial[0]
    for s in range(1, NEAR):
        back_copy[s - 1].wait_recv()
        image = image + landed[s]
    d, r = direction[...], res[...]
    image = outscale[0] * image + jitter[...] * d
    terms = jnp.concatenate([r * r, d * image, r * image, image * image, jnp.zeros((64, SHARD), F32)], axis=0)
    dots_near[0:1, :] = jnp.sum(terms.T, axis=0, keepdims=True)
    one = [
        send(dots_near.at[pl.ds(0, 1)], dots_near.at[pl.ds(s, 1)], one_s.at[s], one_r.at[s], near_to[s])
        for s in range(1, NEAR)
    ]
    for s in (12, 4, 11, 13, 3, 5, 10, 14, 2, 6, 9, 15, 8, 1, 7):
        one[s - 1].start()
    for copy in one:
        copy.wait_recv()
    dots_far[0:1, :] = jnp.sum(dots_near[...], axis=0, keepdims=True)
    two = [
        send(dots_far.at[pl.ds(0, 1)], dots_far.at[pl.ds(s, 1)], two_s.at[s], two_r.at[s], far_to[s])
        for s in range(1, FAR)
    ]
    for s in range(1, FAR):
        two[s - 1].start()
    for copy in two:
        copy.wait_recv()
    sums = jnp.sum(dots_far[...], axis=0, keepdims=True)
    spread = jnp.broadcast_to(sums, (SHARD, SHARD)).T
    rr, dq, rq, qq = [spread[16 * k : 16 * (k + 1)] for k in range(4)]
    alpha = rr / dq
    next_rr = rr + alpha * (alpha * qq - 2.0 * rq)
    updated = r - alpha * image
    new_sol[...] = sol[...] + alpha * d
    new_res[...] = updated
    new_dir[...] = updated + (next_rr / rr) * d
    for copy in near_copy + list(z_copy.values()) + mate_copy + core_copy + back_copy + one + two:
        copy.wait_send()


def per_device(points, lengths, outscale, jitter, sol, res, direction):
    shape = jax.ShapeDtypeStruct((16, SHARD), F32)
    vmem = pl.BlockSpec(memory_space=pltpu.VMEM)
    dma = pltpu.SemaphoreType.DMA
    outs = pl.pallas_call(
        kernel,
        out_shape=(shape, shape, shape),
        in_specs=[vmem, vmem, pl.BlockSpec(memory_space=pltpu.SMEM), vmem, vmem, vmem, vmem],
        out_specs=(vmem, vmem, vmem),
        scratch_shapes=[
            pltpu.VMEM((NEAR, 16, SHARD), F32),
            pltpu.VMEM((FAR, 32, SHARD), F32),
            pltpu.VMEM((DEPTH, NEAR_PTS), BF),
            pltpu.VMEM((FAR * SHARD, DEPTH), BF),
            pltpu.VMEM((32, FAR * SHARD), BF),
            pltpu.VMEM((NEAR, 16, SHARD), F32),
            pltpu.VMEM((NEAR, 16, SHARD), F32),
            pltpu.VMEM((NEAR, SHARD), F32),
            pltpu.VMEM((FAR, SHARD), F32),
            dma((NEAR,)),
            dma((NEAR,)),
            dma((FAR,)),
            dma((FAR,)),
            dma((NEAR,)),
            dma((NEAR,)),
            dma((NEAR,)),
            dma((NEAR,)),
            dma((FAR,)),
            dma((FAR,)),
        ],
        compiler_params=pltpu.CompilerParams(
            collective_id=0, has_side_effects=True, vmem_limit_bytes=48 * 2**20
        ),
        name="cg_step",
    )(
        points.T,
        lengths.reshape(1, 16),
        outscale,
        jitter.reshape(1, SHARD),
        sol.T,
        res.T,
        direction.T,
    )
    return tuple(out.T for out in outs)


def solution(mesh):
    rows = P(("row", "col"), None)
    return jax.shard_map(
        per_device,
        mesh=mesh,
        in_specs=(rows, P(), P(), P(("row", "col")), rows, rows, rows),
        out_specs=(rows, rows, rows),
        check_vma=False,
    )
```

time: 710 us -> 59.7 us (0.08)
  blocking collectives: 346 us -> 0 us
  waiting for transfers between devices: 207 us -> 0 us
  matrix products: 133 us -> 0 us
  Pallas kernels: 0 us -> 53.5 us
  between operations: 14.1 us -> 1.33 us
    reduce_scatter x2 -> x0, waiting for transfers between devices: 206 us -> none  [the longest x1 118 us: per_device(): lax.psum_scatter(back, 'row', scatter_dimension=0, tiled=True)]
    psum x2 -> x0, blocking collectives: 195 us -> none  [the longest x1 100 us: per_device(): norm_now = lax.psum(jnp.sum(residual * residual, axis=0), ('row', 'col'))]
    all_gather x4 -> x0, blocking collectives: 151 us -> none  [the longest x1 48.6 us: per_device(): lax.all_gather(scaled, 'row', axis=0, tiled=True)]
    dot_general x92 -> x0, matrix products: 133 us -> none  [the longest x31 81.9 us: kernel_tile(): jnp.dot(mine, far_scaled.T, precision=lax.Precision.HIGHEST, preferred_el...]
    pallas_call x0 -> x1, Pallas kernels: none -> 53.5 us  [per_device(): pl.pallas_call(kernel, out_shape=(shape, shape, shape), in_specs=[vmem, v...]
  transfers between devices with their start and end apart: 2 -> 0, of which waited for: 2 -> 0; matrix products, arithmetic and copies ran while one was open for 0% -> 0% of each run, Pallas kernels for 0% -> 0%
where the time goes in v1:
time: 59.7 us; the launch traced here: 59.4 us
  Pallas kernels  53.5 us (90%)
  local copies, waits for them, and re-layouts  4.54 us (8%)
  between operations  1.33 us (2%)
    pallas_call x1, Pallas kernels, per_device(): pl.pallas_call(kernel, out_shape=(shape, shape, shape), in_specs=[vmem, v...  53.5 us
    unnamed x15, local copies, waits for them, and re-layouts  4.54 us

profile of v1, /device:TPU:1, one launch (start us, length us, event | category | flops | bytes accessed | tf_op | source)
XLA Modules:
  0.0 59.4 jit_solution(16314856908404173696)
XLA Ops:
  0.6 0.0 copy-start
  1.3 0.0 copy-start.4
  1.3 0.0 copy-start.5
  1.3 0.0 copy-done
  1.3 0.6 %copy-done.4 = f32[16]{0:T(128)S(1)} copy-done((f32[16]{0:T(128)S(1)}, f32[16]{0:T(128)}, u32[]{:S(2)}) %copy-start.4) | copy-done | bytes 88
  2.0 0.0 copy-done.5
  2.0 0.0 copy-start.1
  2.0 0.7 %copy-done.1 = f32[128,16]{0,1:T(8,128)S(1)} copy-done((f32[128,16]{0,1:T(8,128)S(1)}, f32[128,16]{0,1:T(8,128)}, u32[]{:S(2)}) %copy-start.1) | copy-done | bytes 8216
  2.7 0.0 copy-start.2
  2.7 0.7 %copy-done.2 = f32[128,16]{0,1:T(8,128)S(1)} copy-done((f32[128,16]{0,1:T(8,128)S(1)}, f32[128,16]{0,1:T(8,128)}, u32[]{:S(2)}) %copy-start.2) | copy-done | bytes 8216
  3.4 0.0 copy-start.3
  3.4 0.7 %copy-done.3 = f32[128,16]{0,1:T(8,128)S(1)} copy-done((f32[128,16]{0,1:T(8,128)S(1)}, f32[128,16]{0,1:T(8,128)}, u32[]{:S(2)}) %copy-start.3) | copy-done | bytes 8216
  4.1 53.5 %cg_step.1 = (f32[16,128]{1,0:T(8,128)S(1)}, f32[16,128]{1,0:T(8,128)S(1)}, f32[16,128]{1,0:T(8,128)S(1)}) custom-call(f32[16,128]{1,0:T(8,128)S(1)} %bitcast.12, f32[1,16]{1,0:T(1,128)S(1)} %bitcast.16, f32[1]{0:T(128)S(6)} %copy.13.outscale, f32[1,128]{1,0:T(1,128)S(1)} %bitcast.17, f32[16,128]{1,0:T(8,128)S(1)} %bitcast.13, f32[16,128]{1,0:T(8,128)S(1)} %bitcast.14, ...), custom_call_target="tpu_custom_call" | custom-call | tf_op jit(solution)/shard_map/cg_step/pallas_call | solution.py:244
  57.6 0.6 %copy.14 = f32[128,16]{0,1:T(8,128)} copy(f32[128,16]{0,1:T(8,128)S(1)} %bitcast.11) | data formatting | bytes 16384
  58.2 0.6 %copy.15 = f32[128,16]{0,1:T(8,128)} copy(f32[128,16]{0,1:T(8,128)S(1)} %bitcast.10) | data formatting | bytes 16384
  58.8 0.6 %copy.16 = f32[128,16]{0,1:T(8,128)} copy(f32[128,16]{0,1:T(8,128)S(1)} %bitcast.9) | data formatting | bytes 16384
Async XLA Ops:
  0.6 0.7 %copy-start = (f32[128,16]{0,1:T(8,128)S(1)}, f32[128,16]{0,1:T(8,128)}, u32[]{:S(2)}) copy-start(f32[128,16]{0,1:T(8,128)} %param.7) | copy-start | bytes 24580
  1.3 0.7 %copy-start.4 = (f32[16]{0:T(128)S(1)}, f32[16]{0:T(128)}, u32[]{:S(2)}) copy-start(f32[16]{0:T(128)} %param.8) | copy-start | bytes 196
  1.3 0.7 %copy-start.5 = (f32[128]{0:T(128)S(1)}, f32[128]{0:T(128)}, u32[]{:S(2)}) copy-start(f32[128]{0:T(128)} %param.10) | copy-start | bytes 1540
  2.0 0.7 %copy-start.1 = (f32[128,16]{0,1:T(8,128)S(1)}, f32[128,16]{0,1:T(8,128)}, u32[]{:S(2)}) copy-start(f32[128,16]{0,1:T(8,128)} %param.11) | copy-start | bytes 24580
  2.7 0.7 %copy-start.2 = (f32[128,16]{0,1:T(8,128)S(1)}, f32[128,16]{0,1:T(8,128)}, u32[]{:S(2)}) copy-start(f32[128,16]{0,1:T(8,128)} %param.12) | copy-start | bytes 24580
  3.4 0.7 %copy-start.3 = (f32[128,16]{0,1:T(8,128)S(1)}, f32[128,16]{0,1:T(8,128)}, u32[]{:S(2)}) copy-start(f32[128,16]{0,1:T(8,128)} %param.13) | copy-start | bytes 24580

commit v2 on v1

v2 whole, which is shorter than its diff:
```python
import math

import jax
import jax.numpy as jnp
from jax import lax
from jax.experimental import pallas as pl
from jax.experimental.pallas import tpu as pltpu
from jax.sharding import PartitionSpec as P

MESH = pl.DeviceIdType.MESH
BF = jnp.bfloat16
F32 = jnp.float32
LOG2E = math.log2(math.e)
DEPTH = 128
NEAR = 16
FAR = 32
SHARD = 128
NEAR_PTS = NEAR * SHARD
CHUNK = 8
LEADERS = 32
DEVICES = 512
HALF = NEAR // 2
STEP = CHUNK * SHARD
WIDE = HALF * SHARD
OFFSETS = (
    (0, 0), (0, 1), (0, 7), (0, 2), (0, 6), (1, 0), (0, 3), (0, 5),
    (1, 1), (1, 7), (1, 2), (1, 6), (0, 4), (1, 3), (1, 5), (1, 4),
)


def split3(x):
    hi = x.astype(BF)
    rest = x - hi.astype(F32)
    mid = rest.astype(BF)
    low = (rest - mid.astype(F32)).astype(BF)
    return hi, mid, low


def augment(u, near):
    hi, mid, low = split3(u)
    half = -0.5 * jnp.sum(u * u, axis=0, keepdims=True)
    h0, h1, h2 = [part.astype(F32) for part in split3(half)]
    row = lax.broadcasted_iota(jnp.int32, u.shape, 0)
    if near:
        ones = jnp.where((row >= 3) & (row < 6), 1.0, 0.0)
        tail = jnp.where(row == 0, h0, jnp.where(row == 1, h1, jnp.where(row == 2, h2, ones)))
        parts = [hi, hi, mid, mid, hi, low]
    else:
        ones = jnp.where(row < 3, 1.0, 0.0)
        tail = jnp.where(row == 3, h0, jnp.where(row == 4, h1, jnp.where(row == 5, h2, ones)))
        parts = [hi, mid, hi, mid, low, hi]
    return jnp.concatenate(parts + [tail.astype(BF), jnp.zeros_like(hi)], axis=0)


def place():
    r, c = lax.axis_index("row"), lax.axis_index("col")
    x, z, core = c // 4, r // 4, lax.rem(r, 2)
    y = lax.rem(c, 4) * 2 + lax.rem(r // 2, 2)
    return x, y, z, core


def device(x, y, z, core):
    return (z * 4 + lax.rem(y, 2) * 2 + core, x * 4 + y // 2)


def kernel(
    points_hbm,
    lengths_hbm,
    outscale_hbm,
    jitter_hbm,
    res_hbm,
    direction_hbm,
    result,
    points,
    lengths,
    outscale,
    jitter,
    res,
    direction,
    load_sem,
    near,
    far,
    near_op,
    far_op,
    dir_op,
    partial,
    landed,
    dots,
    gathered,
    total,
    near_s,
    near_r,
    far_s,
    far_r,
    back_s,
    back_r,
    up_s,
    up_r,
    down_s,
    down_r,
):
    x, y, z, core = place()

    def near_peer(slot, sign):
        dx, dy = OFFSETS[slot]
        dy = dy if sign > 0 else (8 - dy) % 8
        return device(lax.rem(x + 2 * dx, 4), lax.rem(y + dy, 8), z, core)

    def far_peer(q, dz):
        xl, co = q // 2, q % 2
        mate = x + xl * (1 - 2 * lax.rem(x, 2))
        return device(mate, y, lax.rem(z + dz, 8), lax.rem(core + co, 2))

    def send(src, dst, ss, rs, peer):
        return pltpu.make_async_remote_copy(
            src_ref=src, dst_ref=dst, send_sem=ss, recv_sem=rs, device_id=peer, device_id_type=MESH
        )

    near_to = [near_peer(s, 1) for s in range(NEAR)]
    near_from = [near_peer(s, -1) for s in range(NEAR)]
    far_to = [far_peer(q, dz) for q in range(2) for dz in range(8)] + [far_peer(2, 0)]
    leader = (z == 0) & (core == 1)
    me = (z * 2 + core) * 32 + x * 8 + y

    barrier = pltpu.get_barrier_semaphore()
    for peer in near_to[1:] + far_to[1:]:
        pl.semaphore_signal(barrier, inc=1, device_id=peer, device_id_type=MESH)

    loads = [
        pltpu.make_async_copy(src, dst, load_sem.at[k])
        for k, (src, dst) in enumerate(
            (
                (points_hbm, points),
                (lengths_hbm, lengths),
                (direction_hbm, direction),
                (outscale_hbm, outscale),
                (jitter_hbm, jitter),
                (res_hbm, res),
            )
        )
    ]
    for load in loads:
        load.start()
    pending = []

    def go(copy):
        copy.start()
        pending.append(copy)

    for load in loads[:3]:
        load.wait()

    eye = lax.broadcasted_iota(jnp.int32, (16, 16), 0) == lax.broadcasted_iota(jnp.int32, (16, 16), 1)
    column = jnp.sum(jnp.where(eye, jnp.broadcast_to(lengths[...], (16, 16)), 0.0), axis=1, keepdims=True)
    mine = points[...] * (math.sqrt(LOG2E) / column)
    near[0] = mine
    far[0, :16] = mine
    far[0, 16:] = direction[...]

    pl.semaphore_wait(barrier, len(near_to) + len(far_to) - 2)

    order = (4, 3, 5, 2, 6, 1, 7)
    z_copy = {
        dz: send(far.at[0], far.at[dz], far_s.at[dz], far_r.at[dz], far_to[dz]) for dz in order
    }
    mate_copy = [
        send(far.at[dz], far.at[16 + dz], far_s.at[16 + dz], far_r.at[16 + dz], far_to[16]) for dz in range(8)
    ]
    core_copy = [
        send(far.at[k], far.at[k + 8], far_s.at[k + 8], far_r.at[k + 8], far_to[8])
        for k in list(range(8)) + list(range(16, 24))
    ]
    near_copy = [
        send(near.at[0], near.at[s], near_s.at[s], near_r.at[s], near_to[s]) for s in range(1, NEAR)
    ]
    for s in range(1, HALF):
        go(near_copy[s - 1])
    for dz in order:
        go(z_copy[dz])
    go(mate_copy[0])
    go(core_copy[0])
    for s in reversed(range(HALF, NEAR)):
        go(near_copy[s - 1])

    def prepare_near(s, carry):
        near_op[:, pl.ds(pl.multiple_of(s * SHARD, SHARD), SHARD)] = augment(near[s], True)
        return carry

    def prepare_far(k, carry):
        here = pl.ds(pl.multiple_of(k * SHARD, SHARD), SHARD)
        far_op[here, :] = augment(far[k, :16], False).T
        d = far[k, 16:]
        hi = d.astype(BF)
        dir_op[:, here] = jnp.concatenate([hi, (d - hi.astype(F32)).astype(BF)], axis=0)
        return carry

    for copy in near_copy[: HALF - 1]:
        copy.wait_recv()
    lax.fori_loop(0, HALF, prepare_near, 0)
    for dz in reversed(order):
        z_copy[dz].wait_recv()
        go(mate_copy[dz])
        go(core_copy[dz])
    lax.fori_loop(0, CHUNK, prepare_far, 0)

    back_copy = [
        send(partial.at[s], landed.at[s], back_s.at[s], back_r.at[s], near_from[s]) for s in range(1, NEAR)
    ]

    def step(t, carry):
        @pl.when(t == 1)
        def _():
            for copy in near_copy[HALF - 1 :]:
                copy.wait_recv()
            lax.fori_loop(HALF, NEAR, prepare_near, 0)

        @pl.when(t == 2)
        def _():
            for k in range(CHUNK):
                core_copy[k].wait_recv()
            lax.fori_loop(CHUNK, 2 * CHUNK, prepare_far, 0)

        @pl.when(t == 4)
        def _():
            for k in range(CHUNK):
                mate_copy[k].wait_recv()
                core_copy[CHUNK + k].start()
            lax.fori_loop(2 * CHUNK, 3 * CHUNK, prepare_far, 0)

        @pl.when(t == 5)
        def _():
            for k in range(CHUNK):
                core_copy[CHUNK + k].wait_recv()
            lax.fori_loop(3 * CHUNK, 4 * CHUNK, prepare_far, 0)

        @pl.when(t == 6)
        def _():
            for s in reversed(range(HALF, NEAR)):
                back_copy[s - 1].start()

        late = t // 4
        q = (1 - late) * (t // 2) + late * (2 + lax.rem(t, 2))
        h = (1 - late) * lax.rem(t, 2) + late * (3 - t // 2)
        rows = pl.ds(pl.multiple_of(q * STEP, STEP), STEP)
        columns = pl.ds(pl.multiple_of(h * WIDE, WIDE), WIDE)
        power = jnp.dot(far_op[rows, :], near_op[:, columns], preferred_element_type=F32)
        value = jnp.exp2(power)
        high = value.astype(BF)
        low = (value - high.astype(F32)).astype(BF)
        d = dir_op[:, rows]
        a = jnp.dot(d, high, preferred_element_type=F32)
        b = jnp.dot(d[:16], low, preferred_element_type=F32)
        product = a[:16] + (a[16:] + b)
        for s in range(HALF):
            piece = product[:, s * SHARD : (s + 1) * SHARD]
            slot = h * HALF + s
            partial[slot] = jnp.where(t < 2, piece, partial[slot] + piece)
        return carry

    lax.fori_loop(0, 8, step, 0)
    pending.extend(core_copy[CHUNK:] + back_copy[HALF - 1 :])
    for s in reversed(range(1, HALF)):
        go(back_copy[s - 1])
    image = partial[0]
    for s in range(1, NEAR):
        back_copy[s - 1].wait_recv()
        image = image + landed[s]
    for load in loads[3:]:
        load.wait()
    d, r = direction[...], res[...]
    image = outscale[0] * image + jitter[...] * d
    terms = jnp.concatenate([r * r, d * image, r * image, image * image, jnp.zeros((64, SHARD), F32)], axis=0)
    dots[0:1, :] = jnp.sum(terms.T, axis=0, keepdims=True)
    slot = gathered.at[pl.ds(me, 1)]
    row = dots.at[pl.ds(0, 1)]
    up = [
        send(row, slot, up_s.at[k], up_r, device(lax.rem(x + k // 8, 4), lax.rem(y + k % 8, 8), 0, 1))
        for k in range(LEADERS)
    ]
    for k in range(1, LEADERS):
        go(up[k])
    down = [
        send(total.at[pl.ds(0, 1)], total.at[pl.ds(0, 1)], down_s.at[k], down_r, device(x, y, k // 2, 1 - k % 2))
        for k in range(1, FAR // 2)
    ]

    @pl.when(leader)
    def _():
        own = pltpu.make_async_copy(row, slot, up_r)
        own.start()
        pltpu.make_async_copy(gathered, gathered, up_r).wait()
        total[0:1, :] = jnp.sum(gathered[...], axis=0, keepdims=True)
        for copy in down:
            copy.start()
        for copy in down:
            copy.wait_send()

    @pl.when(jnp.logical_not(leader))
    def _():
        up[0].start()
        down[0].wait_recv()
        up[0].wait_send()

    sums = total[0:1, :]
    spread = jnp.broadcast_to(sums, (SHARD, SHARD)).T
    rr, dq, rq, qq = [spread[16 * k : 16 * (k + 1)] for k in range(4)]
    alpha = rr / dq
    next_rr = rr + alpha * (alpha * qq - 2.0 * rq)
    result[0:16, :] = image
    result[16:32, :] = alpha
    result[32:48, :] = next_rr / rr
    for copy in pending:
        copy.wait_send()


def per_device(points, lengths, outscale, jitter, sol, res, direction):
    vmem = pl.BlockSpec(memory_space=pltpu.VMEM)
    dma = pltpu.SemaphoreType.DMA
    hbm = pl.BlockSpec(memory_space=pltpu.HBM)
    result = pl.pallas_call(
        kernel,
        out_shape=jax.ShapeDtypeStruct((48, SHARD), F32),
        in_specs=[hbm] * 6,
        out_specs=vmem,
        scratch_shapes=[
            pltpu.VMEM((16, SHARD), F32),
            pltpu.VMEM((1, 16), F32),
            pltpu.SMEM((1,), F32),
            pltpu.VMEM((1, SHARD), F32),
            pltpu.VMEM((16, SHARD), F32),
            pltpu.VMEM((16, SHARD), F32),
            dma((6,)),
            pltpu.VMEM((NEAR, 16, SHARD), F32),
            pltpu.VMEM((FAR, 32, SHARD), F32),
            pltpu.VMEM((DEPTH, NEAR_PTS), BF),
            pltpu.VMEM((FAR * SHARD, DEPTH), BF),
            pltpu.VMEM((32, FAR * SHARD), BF),
            pltpu.VMEM((NEAR, 16, SHARD), F32),
            pltpu.VMEM((NEAR, 16, SHARD), F32),
            pltpu.VMEM((8, SHARD), F32),
            pltpu.VMEM((DEVICES, SHARD), F32),
            pltpu.VMEM((8, SHARD), F32),
            dma((NEAR,)),
            dma((NEAR,)),
            dma((FAR,)),
            dma((FAR,)),
            dma((NEAR,)),
            dma((NEAR,)),
            dma((LEADERS,)),
            dma,
            dma((FAR // 2,)),
            dma,
        ],
        compiler_params=pltpu.CompilerParams(
            collective_id=0, has_side_effects=True, vmem_limit_bytes=63 * 2**20
        ),
        name="cg_step",
    )(
        points.T,
        lengths.reshape(1, 16),
        outscale,
        jitter.reshape(1, SHARD),
        res.T,
        direction.T,
    )
    image, alpha, beta = [result[16 * k : 16 * (k + 1)].T for k in range(3)]
    new_res = res - alpha * image
    return sol + alpha * direction, new_res, new_res + beta * direction


def solution(mesh):
    rows = P(("row", "col"), None)
    return jax.shard_map(
        per_device,
        mesh=mesh,
        in_specs=(rows, P(), P(), P(("row", "col")), rows, rows, rows),
        out_specs=(rows, rows, rows),
        check_vma=False,
    )
```

time: 59.7 us -> 52.8 us (0.88)
  local copies, waits for them, and re-layouts: 4.54 us -> 0.01 us
  Pallas kernels: 53.5 us -> 49.9 us
  other arithmetic: 0 us -> 1.34 us
    unnamed x15 -> x6, local copies, waits for them, and re-layouts: 4.54 us -> 0.01 us
    pallas_call x1, Pallas kernels: 53.5 us -> 49.9 us  [per_device(): pl.pallas_call(kernel, out_shape=jax.ShapeDtypeStruct((48, SHARD), F32),...]
    add x0 -> x1, other arithmetic: none -> 1.34 us  [per_device(): return (sol + alpha * direction, new_res, new_res + beta * direction)]
where the time goes in v2:
time: 52.8 us; the launch traced here: 52.6 us
  Pallas kernels  49.9 us (95%)
  other arithmetic  1.34 us (3%)
  between operations  1.33 us (3%)
    pallas_call x1, Pallas kernels, per_device(): pl.pallas_call(kernel, out_shape=jax.ShapeDtypeStruct((48, SHARD), F32),...  49.9 us
    add x1, other arithmetic, per_device(): return (sol + alpha * direction, new_res, new_res + beta * direction)  1.34 us

profile of v2, /device:TPU:1, one launch (start us, length us, event | category | flops | bytes accessed | tf_op | source)
XLA Modules:
  0.0 52.6 jit_solution(9919430012112050179)
XLA Ops:
  1.3 0.0 copy-start
  1.3 0.0 copy-start.1
  1.3 0.0 copy-start.2
  1.3 49.9 %cg_step.1 = f32[48,128]{1,0:T(8,128)} custom-call(f32[16,128]{1,0:T(8,128)} %bitcast.22, f32[1,16]{1,0:T(1,128)} %bitcast.23, f32[1]{0:T(128)S(6)} %copy.10.outscale_hbm, f32[1,128]{1,0:T(1,128)} %bitcast.24, f32[16,128]{1,0:T(8,128)} %bitcast.21, f32[16,128]{1,0:T(8,128)} %bitcast.20), custom_call_target="tpu_custom_call" | custom-call | tf_op jit(solution)/shard_map/cg_step/pallas_call | solution.py:320
  51.2 0.0 copy-done
  51.2 0.0 copy-done.1
  51.3 0.0 copy-done.2
  51.3 1.3 %fusion = (f32[128,16]{0,1:T(8,128)}, f32[128,16]{0,1:T(8,128)}, f32[128,16]{0,1:T(8,128)}) fusion(f32[128,16]{0,1:T(8,128)S(1)} %copy-done, f32[48,128]{1,0:T(8,128)} %cg_step.1, f32[128,16]{0,1:T(8,128)S(1)} %copy-done.1, f32[128,16]{0,1:T(8,128)S(1)} %copy-done.2), kind=kLoop, calls=%fused_computation.1 | loop fusion | flops 12288 | bytes 73728 | tf_op jit(solution)/shard_map/add | solution.py:368
Async XLA Ops:
  1.3 50.0 %copy-start = (f32[128,16]{0,1:T(8,128)S(1)}, f32[128,16]{0,1:T(8,128)}, u32[]{:S(2)}) copy-start(f32[128,16]{0,1:T(8,128)} %param.13) | copy-start | bytes 24580
  1.3 50.0 %copy-start.1 = (f32[128,16]{0,1:T(8,128)S(1)}, f32[128,16]{0,1:T(8,128)}, u32[]{:S(2)}) copy-start(f32[128,16]{0,1:T(8,128)} %param.12) | copy-start | bytes 24580
  1.3 50.0 %copy-start.2 = (f32[128,16]{0,1:T(8,128)S(1)}, f32[128,16]{0,1:T(8,128)}, u32[]{:S(2)}) copy-start(f32[128,16]{0,1:T(8,128)} %param.11) | copy-start | bytes 24580

commit v3 on v2

--- a/solution.py
+++ b/solution.py
@@ -22,11 +22,18 @@
 HALF = NEAR // 2
 STEP = CHUNK * SHARD
 WIDE = HALF * SHARD
-OFFSETS = (
-    (0, 0), (0, 1), (0, 7), (0, 2), (0, 6), (1, 0), (0, 3), (0, 5),
-    (1, 1), (1, 7), (1, 2), (1, 6), (0, 4), (1, 3), (1, 5), (1, 4),
+NEAR_AT = (
+    (0, 0), (1, 0), (7, 0), (0, 1), (1, 1), (7, 1), (2, 0), (6, 0),
+    (3, 0), (5, 0), (2, 1), (6, 1), (4, 0), (3, 1), (5, 1), (4, 1),
 )
-
+FAR_AT = (
+    (0, 0, 0), (0, 1, 0), (0, 3, 0), (1, 0, 0), (3, 0, 0), (0, 2, 0), (0, 0, 1), (0, 1, 1),
+    (0, 3, 1), (0, 2, 1), (1, 0, 1), (3, 0, 1), (2, 0, 0), (2, 0, 1), (1, 1, 0), (3, 3, 0),
+    (1, 3, 0), (3, 1, 0), (1, 2, 0), (3, 2, 0), (1, 1, 1), (3, 3, 1), (2, 1, 0), (2, 3, 0),
+    (2, 2, 0), (1, 3, 1), (3, 1, 1), (1, 2, 1), (3, 2, 1), (2, 1, 1), (2, 3, 1), (2, 2, 1),
+)
+SLOT = {at: k for k, at in enumerate(FAR_AT)}
+LINES = ((0, 1), (0, 3), (1, 0), (3, 0), (0, 2), (2, 0))
 
 def split3(x):
     hi = x.astype(BF)
@@ -54,13 +61,13 @@
 
 def place():
     r, c = lax.axis_index("row"), lax.axis_index("col")
-    x, z, core = c // 4, r // 4, lax.rem(r, 2)
-    y = lax.rem(c, 4) * 2 + lax.rem(r // 2, 2)
+    x, z, core = c >> 2, r >> 2, r & 1
+    y = (c & 3) * 2 + ((r >> 1) & 1)
     return x, y, z, core
 
 
 def device(x, y, z, core):
-    return (z * 4 + lax.rem(y, 2) * 2 + core, x * 4 + y // 2)
+    return (z * 4 + (y & 1) * 2 + core, x * 4 + (y >> 1))
 
 
 def kernel(
@@ -102,14 +109,11 @@
     x, y, z, core = place()
 
     def near_peer(slot, sign):
-        dx, dy = OFFSETS[slot]
-        dy = dy if sign > 0 else (8 - dy) % 8
-        return device(lax.rem(x + 2 * dx, 4), lax.rem(y + dy, 8), z, core)
-
-    def far_peer(q, dz):
-        xl, co = q // 2, q % 2
-        mate = x + xl * (1 - 2 * lax.rem(x, 2))
-        return device(mate, y, lax.rem(z + dz, 8), lax.rem(core + co, 2))
+        dy, dz = NEAR_AT[slot]
+        return device(x, (y + sign * dy) & 7, z ^ dz, core)
+
+    def far_peer(a, b, c):
+        return device((x + b) & 3, y, (z + 2 * a) & 7, core ^ c)
 
     def send(src, dst, ss, rs, peer):
         return pltpu.make_async_remote_copy(
@@ -118,12 +122,14 @@
 
     near_to = [near_peer(s, 1) for s in range(NEAR)]
     near_from = [near_peer(s, -1) for s in range(NEAR)]
-    far_to = [far_peer(q, dz) for q in range(2) for dz in range(8)] + [far_peer(2, 0)]
+    line_to = [far_peer(a, b, 0) for a, b in LINES]
+    mate = far_peer(0, 0, 1)
     leader = (z == 0) & (core == 1)
     me = (z * 2 + core) * 32 + x * 8 + y
 
     barrier = pltpu.get_barrier_semaphore()
-    for peer in near_to[1:] + far_to[1:]:
+    greeted = line_to + near_to[:0:-1] + [mate]
+    for peer in greeted:
         pl.semaphore_signal(barrier, inc=1, device_id=peer, device_id_type=MESH)
 
     loads = [
@@ -157,52 +163,59 @@
     far[0, :16] = mine
     far[0, 16:] = direction[...]
 
-    pl.semaphore_wait(barrier, len(near_to) + len(far_to) - 2)
-
-    order = (4, 3, 5, 2, 6, 1, 7)
-    z_copy = {
-        dz: send(far.at[0], far.at[dz], far_s.at[dz], far_r.at[dz], far_to[dz]) for dz in order
+    pl.semaphore_wait(barrier, len(greeted))
+
+    def far_copy(source, at, peer):
+        k = SLOT[at]
+        return send(far.at[SLOT[source]], far.at[k], far_s.at[k], far_r.at[k], peer)
+
+    line = {(a, b): far_copy((0, 0, 0), (a, b, 0), peer) for (a, b), peer in zip(LINES, line_to)}
+    corner = {
+        (a, b): far_copy((a, 0, 0), (a, b, 0), far_peer(0, b, 0)) for a in (1, 2, 3) for b in (1, 2, 3)
     }
-    mate_copy = [
-        send(far.at[dz], far.at[16 + dz], far_s.at[16 + dz], far_r.at[16 + dz], far_to[16]) for dz in range(8)
-    ]
-    core_copy = [
-        send(far.at[k], far.at[k + 8], far_s.at[k + 8], far_r.at[k + 8], far_to[8])
-        for k in list(range(8)) + list(range(16, 24))
-    ]
+    across = {(a, b): far_copy((a, b, 0), (a, b, 1), mate) for a in range(4) for b in range(4)}
     near_copy = [
         send(near.at[0], near.at[s], near_s.at[s], near_r.at[s], near_to[s]) for s in range(1, NEAR)
     ]
     for s in range(1, HALF):
         go(near_copy[s - 1])
-    for dz in order:
-        go(z_copy[dz])
-    go(mate_copy[0])
-    go(core_copy[0])
+    for at in LINES:
+        go(line[at])
+    go(across[0, 0])
     for s in reversed(range(HALF, NEAR)):
         go(near_copy[s - 1])
 
-    def prepare_near(s, carry):
-        near_op[:, pl.ds(pl.multiple_of(s * SHARD, SHARD), SHARD)] = augment(near[s], True)
-        return carry
-
-    def prepare_far(k, carry):
-        here = pl.ds(pl.multiple_of(k * SHARD, SHARD), SHARD)
-        far_op[here, :] = augment(far[k, :16], False).T
-        d = far[k, 16:]
-        hi = d.astype(BF)
-        dir_op[:, here] = jnp.concatenate([hi, (d - hi.astype(F32)).astype(BF)], axis=0)
-        return carry
+    def prepare_near(h):
+        for s in range(h * HALF, h * HALF + HALF):
+            near_op[:, s * SHARD : (s + 1) * SHARD] = augment(near[s], True)
+
+    def prepare_far(q):
+        for k in range(q * CHUNK, q * CHUNK + CHUNK):
+            here = slice(k * SHARD, (k + 1) * SHARD)
+            far_op[here, :] = augment(far[k, :16], False).T
+            d = far[k, 16:]
+            hi = d.astype(BF)
+            dir_op[:, here] = jnp.concatenate([hi, (d - hi.astype(F32)).astype(BF)], axis=0)
 
     for copy in near_copy[: HALF - 1]:
         copy.wait_recv()
-    lax.fori_loop(0, HALF, prepare_near, 0)
-    for dz in reversed(order):
-        z_copy[dz].wait_recv()
-        go(mate_copy[dz])
-        go(core_copy[dz])
-    lax.fori_loop(0, CHUNK, prepare_far, 0)
-
+    prepare_near(0)
+    for at in ((0, 1), (0, 3)):
+        line[at].wait_recv()
+        go(across[at])
+    for at in ((1, 0), (3, 0)):
+        line[at].wait_recv()
+    for at in ((1, 1), (3, 3), (1, 3), (3, 1), (1, 2), (3, 2)):
+        go(corner[at])
+    for at in ((1, 0), (3, 0)):
+        go(across[at])
+    line[0, 2].wait_recv()
+    go(across[0, 2])
+    across[0, 0].wait_recv()
+    across[0, 1].wait_recv()
+    prepare_far(0)
+
+    later = [corner[2, 1], corner[2, 3], corner[2, 2], across[2, 0]]
     back_copy = [
         send(partial.at[s], landed.at[s], back_s.at[s], back_r.at[s], near_from[s]) for s in range(1, NEAR)
     ]
@@ -210,28 +223,42 @@
     def step(t, carry):
         @pl.when(t == 1)
         def _():
+            line[2, 0].wait_recv()
+            for copy in later:
+                copy.start()
             for copy in near_copy[HALF - 1 :]:
                 copy.wait_recv()
-            lax.fori_loop(HALF, NEAR, prepare_near, 0)
+            prepare_near(1)
 
         @pl.when(t == 2)
         def _():
-            for k in range(CHUNK):
-                core_copy[k].wait_recv()
-            lax.fori_loop(CHUNK, 2 * CHUNK, prepare_far, 0)
+            for at in ((1, 1), (3, 3)):
+                corner[at].wait_recv()
+                across[at].start()
+            for at in ((0, 3), (0, 2), (1, 0), (3, 0), (2, 0)):
+                across[at].wait_recv()
+            prepare_far(1)
+
+        @pl.when(t == 3)
+        def _():
+            for at in ((1, 3), (3, 1), (1, 2), (3, 2)):
+                corner[at].wait_recv()
+                across[at].start()
 
         @pl.when(t == 4)
         def _():
-            for k in range(CHUNK):
-                mate_copy[k].wait_recv()
-                core_copy[CHUNK + k].start()
-            lax.fori_loop(2 * CHUNK, 3 * CHUNK, prepare_far, 0)
+            for at in ((2, 1), (2, 3), (2, 2)):
+                corner[at].wait_recv()
+                across[at].start()
+            for at in ((1, 1), (3, 3)):
+                across[at].wait_recv()
+            prepare_far(2)
 
         @pl.when(t == 5)
         def _():
-            for k in range(CHUNK):
-                core_copy[CHUNK + k].wait_recv()
-            lax.fori_loop(3 * CHUNK, 4 * CHUNK, prepare_far, 0)
+            for a, b, c in FAR_AT[25:]:
+                across[a, b].wait_recv()
+            prepare_far(3)
 
         @pl.when(t == 6)
         def _():
@@ -258,7 +285,7 @@
         return carry
 
     lax.fori_loop(0, 8, step, 0)
-    pending.extend(core_copy[CHUNK:] + back_copy[HALF - 1 :])
+    pending.extend(later + [across[at] for at in corner] + back_copy[HALF - 1 :])
     for s in reversed(range(1, HALF)):
         go(back_copy[s - 1])
     image = partial[0]
@@ -274,7 +301,7 @@
     slot = gathered.at[pl.ds(me, 1)]
     row = dots.at[pl.ds(0, 1)]
     up = [
-        send(row, slot, up_s.at[k], up_r, device(lax.rem(x + k // 8, 4), lax.rem(y + k % 8, 8), 0, 1))
+        send(row, slot, up_s.at[k], up_r, device((x + k // 8) & 3, (y + k % 8) & 7, 0, 1))
         for k in range(LEADERS)
     ]
     for k in range(1, LEADERS):
@@ -286,20 +313,26 @@
 
     @pl.when(leader)
     def _():
-        own = pltpu.make_async_copy(row, slot, up_r)
-        own.start()
+        pltpu.make_async_copy(row, slot, up_r).start()
+
+    @pl.when(jnp.logical_not(leader))
+    def _():
+        up[0].start()
+        up[0].wait_send()
+
+    for copy in pending:
+        copy.wait_send()
+
+    @pl.when(leader)
+    def _():
         pltpu.make_async_copy(gathered, gathered, up_r).wait()
         total[0:1, :] = jnp.sum(gathered[...], axis=0, keepdims=True)
         for copy in down:
             copy.start()
-        for copy in down:
-            copy.wait_send()
 
     @pl.when(jnp.logical_not(leader))
     def _():
-        up[0].start()
         down[0].wait_recv()
-        up[0].wait_send()
 
     sums = total[0:1, :]
     spread = jnp.broadcast_to(sums, (SHARD, SHARD)).T
@@ -309,8 +342,10 @@
     result[0:16, :] = image
     result[16:32, :] = alpha
     result[32:48, :] = next_rr / rr
-    for copy in pending:
-        copy.wait_send()
+    @pl.when(leader)
+    def _():
+        for copy in down:
+            copy.wait_send()
 
 
 def per_device(points, lengths, outscale, jitter, sol, res, direction):

time: 52.8 us -> 49.5 us (0.938)
  Pallas kernels: 49.9 us -> 46.6 us
    pallas_call x1, Pallas kernels: 49.9 us -> 46.6 us  [per_device(): pl.pallas_call(kernel, out_shape=jax.ShapeDtypeStruct((48, SHARD), F32),...]
where the time goes in v3:
time: 49.5 us; the launch traced here: 49.2 us
  Pallas kernels  46.6 us (94%)
  other arithmetic  1.34 us (3%)
  between operations  1.33 us (3%)
    pallas_call x1, Pallas kernels, per_device(): pl.pallas_call(kernel, out_shape=jax.ShapeDtypeStruct((48, SHARD), F32),...  46.6 us
    add x1, other arithmetic, per_device(): return (sol + alpha * direction, new_res, new_res + beta * direction)  1.34 us

profile of v3, /device:TPU:1, one launch (start us, length us, event | category | flops | bytes accessed | tf_op | source)
XLA Modules:
  0.0 49.2 jit_solution(9719700372415506668)
XLA Ops:
  1.3 0.0 copy-start
  1.3 0.0 copy-start.1
  1.3 0.0 copy-start.2
  1.3 46.6 %cg_step.1 = f32[48,128]{1,0:T(8,128)} custom-call(f32[16,128]{1,0:T(8,128)} %bitcast.22, f32[1,16]{1,0:T(1,128)} %bitcast.23, f32[1]{0:T(128)S(6)} %copy.10.outscale_hbm, f32[1,128]{1,0:T(1,128)} %bitcast.24, f32[16,128]{1,0:T(8,128)} %bitcast.21, f32[16,128]{1,0:T(8,128)} %bitcast.20), custom_call_target="tpu_custom_call" | custom-call | tf_op jit(solution)/shard_map/cg_step/pallas_call | solution.py:355
  47.9 0.0 copy-done
  47.9 0.0 copy-done.1
  47.9 0.0 copy-done.2
  47.9 1.3 %fusion = (f32[128,16]{0,1:T(8,128)}, f32[128,16]{0,1:T(8,128)}, f32[128,16]{0,1:T(8,128)}) fusion(f32[128,16]{0,1:T(8,128)S(1)} %copy-done, f32[48,128]{1,0:T(8,128)} %cg_step.1, f32[128,16]{0,1:T(8,128)S(1)} %copy-done.1, f32[128,16]{0,1:T(8,128)S(1)} %copy-done.2), kind=kLoop, calls=%fused_computation.1 | loop fusion | flops 12288 | bytes 73728 | tf_op jit(solution)/shard_map/add | solution.py:403
Async XLA Ops:
  1.3 46.6 %copy-start = (f32[128,16]{0,1:T(8,128)S(1)}, f32[128,16]{0,1:T(8,128)}, u32[]{:S(2)}) copy-start(f32[128,16]{0,1:T(8,128)} %param.13) | copy-start | bytes 24580
  1.3 46.6 %copy-start.1 = (f32[128,16]{0,1:T(8,128)S(1)}, f32[128,16]{0,1:T(8,128)}, u32[]{:S(2)}) copy-start(f32[128,16]{0,1:T(8,128)} %param.12) | copy-start | bytes 24580
  1.3 46.6 %copy-start.2 = (f32[128,16]{0,1:T(8,128)S(1)}, f32[128,16]{0,1:T(8,128)}, u32[]{:S(2)}) copy-start(f32[128,16]{0,1:T(8,128)} %param.11) | copy-start | bytes 24580

commit v4 on v3

--- a/solution.py
+++ b/solution.py
@@ -20,8 +20,8 @@
 LEADERS = 32
 DEVICES = 512
 HALF = NEAR // 2
+QUARTER = HALF // 2
 STEP = CHUNK * SHARD
-WIDE = HALF * SHARD
 NEAR_AT = (
     (0, 0), (1, 0), (7, 0), (0, 1), (1, 1), (7, 1), (2, 0), (6, 0),
     (3, 0), (5, 0), (2, 1), (6, 1), (4, 0), (3, 1), (5, 1), (4, 1),
@@ -220,56 +220,9 @@
         send(partial.at[s], landed.at[s], back_s.at[s], back_r.at[s], near_from[s]) for s in range(1, NEAR)
     ]
 
-    def step(t, carry):
-        @pl.when(t == 1)
-        def _():
-            line[2, 0].wait_recv()
-            for copy in later:
-                copy.start()
-            for copy in near_copy[HALF - 1 :]:
-                copy.wait_recv()
-            prepare_near(1)
-
-        @pl.when(t == 2)
-        def _():
-            for at in ((1, 1), (3, 3)):
-                corner[at].wait_recv()
-                across[at].start()
-            for at in ((0, 3), (0, 2), (1, 0), (3, 0), (2, 0)):
-                across[at].wait_recv()
-            prepare_far(1)
-
-        @pl.when(t == 3)
-        def _():
-            for at in ((1, 3), (3, 1), (1, 2), (3, 2)):
-                corner[at].wait_recv()
-                across[at].start()
-
-        @pl.when(t == 4)
-        def _():
-            for at in ((2, 1), (2, 3), (2, 2)):
-                corner[at].wait_recv()
-                across[at].start()
-            for at in ((1, 1), (3, 3)):
-                across[at].wait_recv()
-            prepare_far(2)
-
-        @pl.when(t == 5)
-        def _():
-            for a, b, c in FAR_AT[25:]:
-                across[a, b].wait_recv()
-            prepare_far(3)
-
-        @pl.when(t == 6)
-        def _():
-            for s in reversed(range(HALF, NEAR)):
-                back_copy[s - 1].start()
-
-        late = t // 4
-        q = (1 - late) * (t // 2) + late * (2 + lax.rem(t, 2))
-        h = (1 - late) * lax.rem(t, 2) + late * (3 - t // 2)
+    def tile(q, slot, slots, fresh):
         rows = pl.ds(pl.multiple_of(q * STEP, STEP), STEP)
-        columns = pl.ds(pl.multiple_of(h * WIDE, WIDE), WIDE)
+        columns = pl.ds(pl.multiple_of(slot * SHARD, slots * SHARD), slots * SHARD)
         power = jnp.dot(far_op[rows, :], near_op[:, columns], preferred_element_type=F32)
         value = jnp.exp2(power)
         high = value.astype(BF)
@@ -278,16 +231,67 @@
         a = jnp.dot(d, high, preferred_element_type=F32)
         b = jnp.dot(d[:16], low, preferred_element_type=F32)
         product = a[:16] + (a[16:] + b)
-        for s in range(HALF):
+        for s in range(slots):
             piece = product[:, s * SHARD : (s + 1) * SHARD]
-            slot = h * HALF + s
-            partial[slot] = jnp.where(t < 2, piece, partial[slot] + piece)
+            partial[slot + s] = piece + (partial[slot + s] if fresh is False else jnp.where(fresh, 0.0, partial[slot + s]))
+
+    def step(t, carry):
+        @pl.when(t == 1)
+        def _():
+            line[2, 0].wait_recv()
+            for copy in later:
+                copy.start()
+            for copy in near_copy[HALF - 1 :]:
+                copy.wait_recv()
+            prepare_near(1)
+
+        @pl.when(t == 2)
+        def _():
+            for at in ((1, 1), (3, 3)):
+                corner[at].wait_recv()
+                across[at].start()
+            for at in ((0, 3), (0, 2), (1, 0), (3, 0), (2, 0)):
+                across[at].wait_recv()
+            prepare_far(1)
+
+        @pl.when(t == 3)
+        def _():
+            for at in ((1, 3), (3, 1), (1, 2), (3, 2)):
+                corner[at].wait_recv()
+                across[at].start()
+
+        @pl.when(t == 4)
+        def _():
+            for at in ((2, 1), (2, 3), (2, 2)):
+                corner[at].wait_recv()
+                across[at].start()
+            for at in ((1, 1), (3, 3)):
+                across[at].wait_recv()
+            prepare_far(2)
+
+        @pl.when(t == 5)
+        def _():
+            for a, b, c in FAR_AT[25:]:
+                across[a, b].wait_recv()
+            prepare_far(3)
+
+        @pl.when(t == 6)
+        def _():
+            for s in reversed(range(HALF, NEAR)):
+                back_copy[s - 1].start()
+
+        late = t // 4
+        q = (1 - late) * (t // 2) + late * (2 + lax.rem(t, 2))
+        h = (1 - late) * lax.rem(t, 2) + late * (3 - t // 2)
+        tile(q, h * HALF, HALF, t < 2)
         return carry
 
-    lax.fori_loop(0, 8, step, 0)
-    pending.extend(later + [across[at] for at in corner] + back_copy[HALF - 1 :])
-    for s in reversed(range(1, HALF)):
-        go(back_copy[s - 1])
+    lax.fori_loop(0, 7, step, 0)
+    for first in (QUARTER, 0):
+        tile(3, first, QUARTER, False)
+        for k in reversed(range(max(first, 1), first + QUARTER)):
+            back_copy[k - 1].start()
+    pending.extend(later + [across[at] for at in corner] + back_copy)
     image = partial[0]
     for s in range(1, NEAR):
         back_copy[s - 1].wait_recv()

time: 49.5 us -> 49.2 us (level)
  no operation moved by 1% of the time
where the time goes in v4:
time: 49.2 us; the launch traced here: 48.9 us
  Pallas kernels  46.2 us (94%)
  other arithmetic  1.34 us (3%)
  between operations  1.33 us (3%)
    pallas_call x1, Pallas kernels, per_device(): pl.pallas_call(kernel, out_shape=jax.ShapeDtypeStruct((48, SHARD), F32),...  46.2 us
    add x1, other arithmetic, per_device(): return (sol + alpha * direction, new_res, new_res + beta * direction)  1.34 us

profile of v4, /device:TPU:1, one launch (start us, length us, event | category | flops | bytes accessed | tf_op | source)
XLA Modules:
  0.0 48.9 jit_solution(1408247653002648185)
XLA Ops:
  1.3 0.0 copy-start
  1.3 0.0 copy-start.1
  1.3 0.0 copy-start.2
  1.3 46.2 %cg_step.1 = f32[48,128]{1,0:T(8,128)} custom-call(f32[16,128]{1,0:T(8,128)} %bitcast.22, f32[1,16]{1,0:T(1,128)} %bitcast.23, f32[1]{0:T(128)S(6)} %copy.10.outscale_hbm, f32[1,128]{1,0:T(1,128)} %bitcast.24, f32[16,128]{1,0:T(8,128)} %bitcast.21, f32[16,128]{1,0:T(8,128)} %bitcast.20), custom_call_target="tpu_custom_call" | custom-call | tf_op jit(solution)/shard_map/cg_step/pallas_call | solution.py:359
  47.6 0.0 copy-done
  47.6 0.0 copy-done.1
  47.6 0.0 copy-done.2
  47.6 1.3 %fusion = (f32[128,16]{0,1:T(8,128)}, f32[128,16]{0,1:T(8,128)}, f32[128,16]{0,1:T(8,128)}) fusion(f32[128,16]{0,1:T(8,128)S(1)} %copy-done, f32[48,128]{1,0:T(8,128)} %cg_step.1, f32[128,16]{0,1:T(8,128)S(1)} %copy-done.1, f32[128,16]{0,1:T(8,128)S(1)} %copy-done.2), kind=kLoop, calls=%fused_computation.1 | loop fusion | flops 12288 | bytes 73728 | tf_op jit(solution)/shard_map/add | solution.py:407
Async XLA Ops:
  1.3 46.3 %copy-start = (f32[128,16]{0,1:T(8,128)S(1)}, f32[128,16]{0,1:T(8,128)}, u32[]{:S(2)}) copy-start(f32[128,16]{0,1:T(8,128)} %param.13) | copy-start | bytes 24580
  1.3 46.3 %copy-start.1 = (f32[128,16]{0,1:T(8,128)S(1)}, f32[128,16]{0,1:T(8,128)}, u32[]{:S(2)}) copy-start(f32[128,16]{0,1:T(8,128)} %param.12) | copy-start | bytes 24580
  1.3 46.3 %copy-start.2 = (f32[128,16]{0,1:T(8,128)S(1)}, f32[128,16]{0,1:T(8,128)}, u32[]{:S(2)}) copy-start(f32[128,16]{0,1:T(8,128)} %param.11) | copy-start | bytes 24580

commit v5 on v4

--- a/solution.py
+++ b/solution.py
@@ -358,7 +358,7 @@
     hbm = pl.BlockSpec(memory_space=pltpu.HBM)
     result = pl.pallas_call(
         kernel,
-        out_shape=jax.ShapeDtypeStruct((48, SHARD), F32),
+        out_shape=pltpu.VMEM((48, SHARD), F32),
         in_specs=[hbm] * 6,
         out_specs=vmem,
         scratch_shapes=[

time: 49.2 us -> 47.8 us (0.972)
  other arithmetic: 1.34 us -> 0.61 us
  Pallas kernels: 46.2 us -> 45.6 us
    add x1, other arithmetic: 1.34 us -> 0.61 us  [per_device(): return (sol + alpha * direction, new_res, new_res + beta * direction)]
    pallas_call x1, Pallas kernels: 46.2 us -> 45.6 us  [per_device(): pl.pallas_call(kernel, out_shape=pltpu.VMEM((48, SHARD), F32), in_specs=[...]
where the time goes in v5:
time: 47.8 us; the launch traced here: 47.6 us
  Pallas kernels  45.6 us (95%)
  between operations  1.33 us (3%)
  other arithmetic  0.61 us (1%)
    pallas_call x1, Pallas kernels, per_device(): pl.pallas_call(kernel, out_shape=pltpu.VMEM((48, SHARD), F32), in_specs=[...  45.6 us

profile of v5, /device:TPU:1, one launch (start us, length us, event | category | flops | bytes accessed | tf_op | source)
XLA Modules:
  0.0 47.6 jit_solution(4109080312159994421)
XLA Ops:
  1.3 0.0 copy-start
  1.3 0.0 copy-start.1
  1.3 0.0 copy-start.2
  1.3 45.6 %cg_step.1 = f32[48,128]{1,0:T(8,128)S(1)} custom-call(f32[16,128]{1,0:T(8,128)} %bitcast.22, f32[1,16]{1,0:T(1,128)} %bitcast.23, f32[1]{0:T(128)S(6)} %copy.10.outscale_hbm, f32[1,128]{1,0:T(1,128)} %bitcast.24, f32[16,128]{1,0:T(8,128)} %bitcast.21, f32[16,128]{1,0:T(8,128)} %bitcast.20), custom_call_target="tpu_custom_call" | custom-call | tf_op jit(solution)/shard_map/cg_step/pallas_call | solution.py:359
  47.0 0.0 copy-done
  47.0 0.0 copy-done.1
  47.0 0.0 copy-done.2
  47.0 0.6 %fusion = (f32[128,16]{0,1:T(8,128)}, f32[128,16]{0,1:T(8,128)}, f32[128,16]{0,1:T(8,128)}) fusion(f32[128,16]{0,1:T(8,128)S(1)} %copy-done, f32[48,128]{1,0:T(8,128)S(1)} %cg_step.1, f32[128,16]{0,1:T(8,128)S(1)} %copy-done.1, f32[128,16]{0,1:T(8,128)S(1)} %copy-done.2), kind=kLoop, calls=%fused_computation.1 | loop fusion | flops 12288 | bytes 73728 | tf_op jit(solution)/shard_map/add | solution.py:407
Async XLA Ops:
  1.3 45.7 %copy-start = (f32[128,16]{0,1:T(8,128)S(1)}, f32[128,16]{0,1:T(8,128)}, u32[]{:S(2)}) copy-start(f32[128,16]{0,1:T(8,128)} %param.13) | copy-start | bytes 24580
  1.3 45.7 %copy-start.1 = (f32[128,16]{0,1:T(8,128)S(1)}, f32[128,16]{0,1:T(8,128)}, u32[]{:S(2)}) copy-start(f32[128,16]{0,1:T(8,128)} %param.12) | copy-start | bytes 24580
  1.3 45.7 %copy-start.2 = (f32[128,16]{0,1:T(8,128)S(1)}, f32[128,16]{0,1:T(8,128)}, u32[]{:S(2)}) copy-start(f32[128,16]{0,1:T(8,128)} %param.11) | copy-start | bytes 24580

commit v6 on v5

--- a/solution.py
+++ b/solution.py
@@ -292,14 +292,15 @@
         for k in reversed(range(max(first, 1), first + QUARTER)):
             back_copy[k - 1].start()
     pending.extend(later + [across[at] for at in corner] + back_copy)
-    image = partial[0]
-    for s in range(1, NEAR):
-        back_copy[s - 1].wait_recv()
-        image = image + landed[s]
     for load in loads[3:]:
         load.wait()
     d, r = direction[...], res[...]
-    image = outscale[0] * image + jitter[...] * d
+    noise = jitter[...] * d
+    image = partial[0]
+    for s in (*range(HALF, NEAR), *range(QUARTER, HALF), *range(1, QUARTER)):
+        back_copy[s - 1].wait_recv()
+        image = image + landed[s]
+    image = outscale[0] * image + noise
     terms = jnp.concatenate([r * r, d * image, r * image, image * image, jnp.zeros((64, SHARD), F32)], axis=0)
     dots[0:1, :] = jnp.sum(terms.T, axis=0, keepdims=True)
     slot = gathered.at[pl.ds(me, 1)]

time: 47.8 us -> 47.8 us (level)
  no operation moved by 1% of the time
where the time goes in v6:
time: 47.8 us; the launch traced here: 47.6 us
  Pallas kernels  45.6 us (95%)
  between operations  1.33 us (3%)
  other arithmetic  0.61 us (1%)
    pallas_call x1, Pallas kernels, per_device(): pl.pallas_call(kernel, out_shape=pltpu.VMEM((48, SHARD), F32), in_specs=[...  45.6 us

profile of v6, /device:TPU:1, one launch (start us, length us, event | category | flops | bytes accessed | tf_op | source)
XLA Modules:
  0.0 47.6 jit_solution(5906725434749000629)
XLA Ops:
  1.3 0.0 copy-start
  1.3 0.0 copy-start.1
  1.3 0.0 copy-start.2
  1.3 45.6 %cg_step.1 = f32[48,128]{1,0:T(8,128)S(1)} custom-call(f32[16,128]{1,0:T(8,128)} %bitcast.22, f32[1,16]{1,0:T(1,128)} %bitcast.23, f32[1]{0:T(128)S(6)} %copy.10.outscale_hbm, f32[1,128]{1,0:T(1,128)} %bitcast.24, f32[16,128]{1,0:T(8,128)} %bitcast.21, f32[16,128]{1,0:T(8,128)} %bitcast.20), custom_call_target="tpu_custom_call" | custom-call | tf_op jit(solution)/shard_map/cg_step/pallas_call | solution.py:360
  46.9 0.0 copy-done
  46.9 0.0 copy-done.1
  46.9 0.0 copy-done.2
  47.0 0.6 %fusion = (f32[128,16]{0,1:T(8,128)}, f32[128,16]{0,1:T(8,128)}, f32[128,16]{0,1:T(8,128)}) fusion(f32[128,16]{0,1:T(8,128)S(1)} %copy-done, f32[48,128]{1,0:T(8,128)S(1)} %cg_step.1, f32[128,16]{0,1:T(8,128)S(1)} %copy-done.1, f32[128,16]{0,1:T(8,128)S(1)} %copy-done.2), kind=kLoop, calls=%fused_computation.1 | loop fusion | flops 12288 | bytes 73728 | tf_op jit(solution)/shard_map/add | solution.py:408
Async XLA Ops:
  1.3 45.7 %copy-start = (f32[128,16]{0,1:T(8,128)S(1)}, f32[128,16]{0,1:T(8,128)}, u32[]{:S(2)}) copy-start(f32[128,16]{0,1:T(8,128)} %param.13) | copy-start | bytes 24580
  1.3 45.7 %copy-start.1 = (f32[128,16]{0,1:T(8,128)S(1)}, f32[128,16]{0,1:T(8,128)}, u32[]{:S(2)}) copy-start(f32[128,16]{0,1:T(8,128)} %param.12) | copy-start | bytes 24580
  1.3 45.7 %copy-start.2 = (f32[128,16]{0,1:T(8,128)S(1)}, f32[128,16]{0,1:T(8,128)}, u32[]{:S(2)}) copy-start(f32[128,16]{0,1:T(8,128)} %param.11) | copy-start | bytes 24580

commit v7 on v6

--- a/solution.py
+++ b/solution.py
@@ -309,8 +309,9 @@
         send(row, slot, up_s.at[k], up_r, device((x + k // 8) & 3, (y + k % 8) & 7, 0, 1))
         for k in range(LEADERS)
     ]
-    for k in range(1, LEADERS):
+    for k in sorted(range(1, LEADERS), key=lambda k: -min(k // 8, 4 - k // 8) - min(k % 8, 8 - k % 8)):
         go(up[k])
+    result[0:16, :] = image
     down = [
         send(total.at[pl.ds(0, 1)], total.at[pl.ds(0, 1)], down_s.at[k], down_r, device(x, y, k // 2, 1 - k % 2))
         for k in range(1, FAR // 2)
@@ -344,7 +345,6 @@
     rr, dq, rq, qq = [spread[16 * k : 16 * (k + 1)] for k in range(4)]
     alpha = rr / dq
     next_rr = rr + alpha * (alpha * qq - 2.0 * rq)
-    result[0:16, :] = image
     result[16:32, :] = alpha
     result[32:48, :] = next_rr / rr
     @pl.when(leader)

time: 47.8 us -> 47.6 us (level)
  no operation moved by 1% of the time
where the time goes in v7:
time: 47.6 us; the launch traced here: 47.5 us
  Pallas kernels  45.5 us (96%)
  between operations  1.33 us (3%)
  other arithmetic  0.61 us (1%)
    pallas_call x1, Pallas kernels, per_device(): pl.pallas_call(kernel, out_shape=pltpu.VMEM((48, SHARD), F32), in_specs=[...  45.5 us

profile of v7, /device:TPU:1, one launch (start us, length us, event | category | flops | bytes accessed | tf_op | source)
XLA Modules:
  0.0 47.5 jit_solution(9457101202068693904)
XLA Ops:
  1.3 0.0 copy-start
  1.3 0.0 copy-start.1
  1.3 0.0 copy-start.2
  1.3 45.5 %cg_step.1 = f32[48,128]{1,0:T(8,128)S(1)} custom-call(f32[16,128]{1,0:T(8,128)} %bitcast.22, f32[1,16]{1,0:T(1,128)} %bitcast.23, f32[1]{0:T(128)S(6)} %copy.10.outscale_hbm, f32[1,128]{1,0:T(1,128)} %bitcast.24, f32[16,128]{1,0:T(8,128)} %bitcast.21, f32[16,128]{1,0:T(8,128)} %bitcast.20), custom_call_target="tpu_custom_call" | custom-call | tf_op jit(solution)/shard_map/cg_step/pallas_call | solution.py:360
  46.8 0.0 copy-done
  46.8 0.0 copy-done.1
  46.8 0.0 copy-done.2
  46.8 0.6 %fusion = (f32[128,16]{0,1:T(8,128)}, f32[128,16]{0,1:T(8,128)}, f32[128,16]{0,1:T(8,128)}) fusion(f32[128,16]{0,1:T(8,128)S(1)} %copy-done, f32[48,128]{1,0:T(8,128)S(1)} %cg_step.1, f32[128,16]{0,1:T(8,128)S(1)} %copy-done.1, f32[128,16]{0,1:T(8,128)S(1)} %copy-done.2), kind=kLoop, calls=%fused_computation.1 | loop fusion | flops 12288 | bytes 73728 | tf_op jit(solution)/shard_map/add | solution.py:408
Async XLA Ops:
  1.3 45.5 %copy-start = (f32[128,16]{0,1:T(8,128)S(1)}, f32[128,16]{0,1:T(8,128)}, u32[]{:S(2)}) copy-start(f32[128,16]{0,1:T(8,128)} %param.13) | copy-start | bytes 24580
  1.3 45.5 %copy-start.1 = (f32[128,16]{0,1:T(8,128)S(1)}, f32[128,16]{0,1:T(8,128)}, u32[]{:S(2)}) copy-start(f32[128,16]{0,1:T(8,128)} %param.12) | copy-start | bytes 24580
  1.3 45.5 %copy-start.2 = (f32[128,16]{0,1:T(8,128)S(1)}, f32[128,16]{0,1:T(8,128)}, u32[]{:S(2)}) copy-start(f32[128,16]{0,1:T(8,128)} %param.11) | copy-start | bytes 24580
